TPU v7x, 32 devices: a whole 2x2x4 slice. The times are simulated.
32 devices in a mesh: ctx: 16 (over z, x, core), head: 2 (over y).
Axes of the slice: x: 2, y: 2, z: 4, core: 2. Of those that a mesh axis runs over, the one named last changes fastest.
Arguments:
- queries: bfloat16 [8192, 2048], P('ctx', 'head'), may hold values from -24 to 24
- keys: bfloat16 [8192, 1024], P('ctx', 'head'), may hold values from -6 to 6
- values: bfloat16 [8192, 1024], P('ctx', 'head'), may hold values from -6 to 6
- out_weight: bfloat16 [128, 16, 4608], P(None, 'head'), may hold values from -0.125 to 0.125
- cotangent: bfloat16 [8192, 4608], P(('ctx', 'head')), may hold values from -3 to 3
Outputs:
- query_grad: float32 [8192, 2048], P('ctx', 'head')
- key_grad: float32 [8192, 1024], P('ctx', 'head')
- value_grad: float32 [8192, 1024], P('ctx', 'head')
- weight_grad: float32 [128, 16, 4608], P('ctx', 'head')
All inputs are finite; a program needn't handle non-finite values.
Results may differ from a plain program's by a relative error of at most 0.02.
Values may be sent and summed in bfloat16 or wider, within the bound.
A program may use at most 128 MiB of HBM per device.

v0:
```python
import jax
import jax.numpy as jnp
from jax import lax
from jax.sharding import PartitionSpec as P

WINDOW = 4096
SPAN = 8


SOFT_CAP = 50.0
QUERY_MULTIPLIER = 144.0 ** (-0.5)
ROPE_BASE = 10000.0


def passed_along(block, axis, distance):
    devices = range(lax.axis_size(axis))
    route = [(i - distance, i) for i in devices if i - distance in devices]
    return lax.ppermute(block, axis, route)


def rotary_tables(positions, width):
    half_width = width // 2
    frequency = ROPE_BASE ** (-(jnp.arange(half_width, dtype=jnp.float32) * 2.0) / width)
    angles = positions.astype(jnp.float32)[:, None] * frequency[None, :]
    return (jnp.cos(angles)[:, None, :], jnp.sin(angles)[:, None, :])


def rotate(values_in, cosine, sine_table):
    half_width = values_in.shape[-1] // 2
    first_half = values_in[..., :half_width]
    second_half = values_in[..., half_width:]
    return jnp.concatenate(
        [
            first_half * cosine - second_half * sine_table,
            second_half * cosine + first_half * sine_table,
        ],
        axis=-1,
    )


def unrotate(values_in, cosine, sine_table):
    half_width = values_in.shape[-1] // 2
    first_half = values_in[..., :half_width]
    second_half = values_in[..., half_width:]
    return jnp.concatenate(
        [
            first_half * cosine + second_half * sine_table,
            second_half * cosine - first_half * sine_table,
        ],
        axis=-1,
    )


def weight_reduce(attn_out, full_grad, query_heads, head_dim):
    attn_flat = attn_out.reshape(attn_out.shape[0], query_heads, head_dim)
    full_term = jnp.einsum("the,td->ehd", attn_flat, full_grad, preferred_element_type=jnp.float32)
    return lax.psum_scatter(full_term, "ctx", scatter_dimension=0, tiled=True)


def local(queries, keys, values, out_weight, cotangent):
    tok_rows = queries.shape[0]
    head_dim = out_weight.shape[0]
    query_heads = queries.shape[1] // head_dim
    kv_heads = keys.shape[1] // head_dim
    group_size = query_heads // kv_heads
    first_row = lax.axis_index("ctx") * tok_rows
    positions = first_row + jnp.arange(tok_rows, dtype=jnp.int32)
    cosine, sine_table = rotary_tables(positions, head_dim)
    query_rotated = (
        rotate(
            queries.reshape(tok_rows, query_heads, head_dim).astype(jnp.float32), cosine, sine_table
        )
        .astype(jnp.bfloat16)
        .reshape(tok_rows, kv_heads, group_size, head_dim)
    )
    key_rot = rotate(
        keys.reshape(tok_rows, kv_heads, head_dim).astype(jnp.float32), cosine, sine_table
    ).astype(jnp.bfloat16)
    value_own = values.reshape(tok_rows, kv_heads, head_dim)
    full_grad = lax.all_gather(cotangent, "head", axis=0, tiled=True)
    output_gradient = (
        jnp.einsum("td,ehd->the", full_grad, out_weight, preferred_element_type=jnp.float32)
        .astype(jnp.bfloat16)
        .reshape(tok_rows, kv_heads, group_size, head_dim)
    )
    own_pair = jnp.stack([key_rot, value_own])
    fetched = []
    for distance in range(1, SPAN + 1):
        fetched.append(passed_along(own_pair, "ctx", distance))
    key_tiles = jnp.stack(fetched[::-1] + [own_pair])
    key_first = first_row - SPAN * tok_rows
    tile_ids = jnp.arange(SPAN + 1, dtype=jnp.int32)

    def tile_setup(tile_index, key_panel):
        key_pos = key_first + tile_index * tok_rows + jnp.arange(tok_rows, dtype=jnp.int32)
        offset = positions[:, None] - key_pos[None, :]
        visible = (offset >= 0) & (offset < WINDOW) & (key_pos[None, :] >= 0)
        uncapped_score = (
            jnp.einsum(
                "qfwy,vfy->fwqv", query_rotated, key_panel[0], preferred_element_type=jnp.float32
            )
            * QUERY_MULTIPLIER
        )
        return (visible, jnp.tanh(uncapped_score / SOFT_CAP))

    def forward_tile(state, inputs):
        row_total, weighted_values = state
        tile_index, key_panel = inputs
        visible, tanh_val = tile_setup(tile_index, key_panel)
        exponent_score = jnp.where(visible, jnp.exp(SOFT_CAP * tanh_val), 0.0)
        row_total = row_total + jnp.sum(exponent_score, axis=-1)
        weighted_values = weighted_values + jnp.einsum(
            "fpxe,efv->xfpv",
            exponent_score.astype(jnp.bfloat16),
            key_panel[1],
            preferred_element_type=jnp.float32,
        )
        return ((row_total, weighted_values), None)

    start_state = (
        jnp.zeros((kv_heads, group_size, tok_rows), jnp.float32),
        jnp.zeros((tok_rows, kv_heads, group_size, head_dim), jnp.float32),
    )
    (row_total, weighted_values), unused = lax.scan(
        forward_tile, start_state, (tile_ids, key_tiles)
    )
    attn_out = (weighted_values / jnp.transpose(row_total, (2, 0, 1))[..., None]).astype(
        jnp.bfloat16
    )
    log_total = jnp.log(row_total)
    row_delta = jnp.transpose(
        jnp.sum(output_gradient.astype(jnp.float32) * attn_out.astype(jnp.float32), axis=-1),
        (1, 2, 0),
    )

    def backward_tile(query_acc, inputs):
        tile_index, key_panel = inputs
        visible, tanh_val = tile_setup(tile_index, key_panel)
        softmax_probability = jnp.where(
            visible, jnp.exp(SOFT_CAP * tanh_val - log_total[..., None]), 0.0
        )
        probability_gradient = jnp.einsum(
            "qfwy,vfy->fwqv", output_gradient, key_panel[1], preferred_element_type=jnp.float32
        )
        score_gradient = (
            softmax_probability
            * (probability_gradient - row_delta[..., None])
            * (1.0 - tanh_val * tanh_val)
            * QUERY_MULTIPLIER
        ).astype(jnp.bfloat16)
        query_acc = query_acc + jnp.einsum(
            "fpxe,efv->xfpv", score_gradient, key_panel[0], preferred_element_type=jnp.float32
        )
        key_portion = jnp.einsum(
            "vcfh,fvcx->hvx", score_gradient, query_rotated, preferred_element_type=jnp.float32
        )
        value_portion = jnp.einsum(
            "vcfh,fvcx->hvx",
            softmax_probability.astype(jnp.bfloat16),
            output_gradient,
            preferred_element_type=jnp.float32,
        )
        return (query_acc, jnp.stack([key_portion, value_portion]))

    query_acc, contrib = lax.scan(
        backward_tile,
        jnp.zeros((tok_rows, kv_heads, group_size, head_dim), jnp.float32),
        (tile_ids, key_tiles),
    )
    running = contrib[0]
    for distance in range(SPAN - 1, -1, -1):
        running = passed_along(running, "ctx", -1) + contrib[SPAN - distance]
    query_grad = unrotate(
        query_acc.reshape(tok_rows, query_heads, head_dim), cosine, sine_table
    ).reshape(tok_rows, query_heads * head_dim)
    key_grad = unrotate(running[0], cosine, sine_table).reshape(tok_rows, kv_heads * head_dim)
    value_grad = running[1].reshape(tok_rows, kv_heads * head_dim)
    weight_grad = weight_reduce(attn_out, full_grad, query_heads, head_dim)
    return (query_grad, key_grad, value_grad, weight_grad)


def solution(mesh):
    placed = (
        P("ctx", "head"),
        P("ctx", "head"),
        P("ctx", "head"),
        P(None, "head", None),
        P(("ctx", "head"), None),
    )
    return jax.shard_map(
        local,
        mesh=mesh,
        in_specs=placed,
        out_specs=(P("ctx", "head"), P("ctx", "head"), P("ctx", "head"), P("ctx", "head", None)),
        check_vma=False,
    )
```

profile of v0, /device:TPU:15, one launch (start us, length us, event | category | flops | bytes accessed | tf_op | source)
XLA Modules:
  0.0 865.7 jit_solution(7384379896425302598)
XLA Ops:
  11.7 5.2 collective-permute-start
  30.6 31.4 %collective-permute-done = bf16[2,512,4,128]{1,3,2,0:T(8,128)(2,1)} collective-permute-done((bf16[2,512,4,128]{1,3,2,0:T(8,128)(2,1)}, bf16[2,512,4,128]{1,3,2,0:T(8,128)(2,1)}, u32[]{:S(2)}, u32[]{:S(2)}) %collective-permute-start) | collective-permute-done | bytes 1048608 | tf_op jit(solution)/shard_map/ppermute | solution.py:18
  66.2 141.3 %collective-permute-done.1 = bf16[2,512,4,128]{1,3,2,0:T(8,128)(2,1)} collective-permute-done((bf16[2,512,4,128]{1,3,2,0:T(8,128)(2,1)}, bf16[2,512,4,128]{1,3,2,0:T(8,128)(2,1)}, u32[]{:S(2)}, u32[]{:S(2)}) %collective-permute-start.1) | collective-permute-done | bytes 1048608 | tf_op jit(solution)/shard_map/ppermute | solution.py:18
  218.5 11.6 %collective-permute-done.4 = bf16[2,512,4,128]{1,3,2,0:T(8,128)(2,1)S(1)} collective-permute-done((bf16[2,512,4,128]{1,3,2,0:T(8,128)(2,1)}, bf16[2,512,4,128]{1,3,2,0:T(8,128)(2,1)S(1)}, u32[]{:S(2)}, u32[]{:S(2)}) %collective-permute-start.4) | collective-permute-done | bytes 1048608 | tf_op jit(solution)/shard_map/ppermute | solution.py:18
  231.1 21.4 %collective-permute-done.5 = bf16[2,512,4,128]{1,3,2,0:T(8,128)(2,1)S(1)} collective-permute-done((bf16[2,512,4,128]{1,3,2,0:T(8,128)(2,1)}, bf16[2,512,4,128]{1,3,2,0:T(8,128)(2,1)S(1)}, u32[]{:S(2)}, u32[]{:S(2)}) %collective-permute-start.5) | collective-permute-done | bytes 1048608 | tf_op jit(solution)/shard_map/ppermute | solution.py:18
  253.7 10.2 %collective-permute-done.6 = bf16[2,512,4,128]{1,3,2,0:T(8,128)(2,1)S(1)} collective-permute-done((bf16[2,512,4,128]{1,3,2,0:T(8,128)(2,1)}, bf16[2,512,4,128]{1,3,2,0:T(8,128)(2,1)S(1)}, u32[]{:S(2)}, u32[]{:S(2)}) %collective-permute-start.6) | collective-permute-done | bytes 1048608 | tf_op jit(solution)/shard_map/ppermute | solution.py:18
  268.2 12.8 %copy.34 = bf16[9,2,512,4,128]{4,2,3,1,0:T(8,128)(2,1)} copy(bf16[9,2,512,4,128]{2,4,3,1,0:T(8,128)(2,1)} %bitcast_dynamic-update-slice_fusion) | data formatting | bytes 18874368
  281.1 87.4 %while.30 = (s32[]{:T(128)}, f32[4,2,512]{2,1,0:T(2,128)S(1)}, f32[512,4,2,128]{0,3,2,1:T(8,128)S(1)}, s32[9]{0:T(128)S(1)}, s32[]{:T(128)}, /*index=5*/bf16[9,2...) while((s32[]{:T(128)}, f32[4,2,512]{2,1,0:T(2,128)S(1)}, ...), condition=%wide.region_2.3_spmd.clone, body=%wide.region_0.2_spmd.clone.sunk | while | flops 1092884480 | bytes 23930064 | solution.py:124
  282.7 4.1 fusion.74
  286.8 4.0 bitcast_add_fusion.12
  292.4 4.1 fusion.74
  296.5 4.0 bitcast_add_fusion.12
  302.1 4.1 fusion.74
  306.2 4.0 bitcast_add_fusion.12
  311.8 4.1 fusion.74
  315.9 4.0 bitcast_add_fusion.12
  321.5 4.1 fusion.74
  325.6 4.0 bitcast_add_fusion.12
  331.2 4.1 fusion.74
  335.3 4.0 bitcast_add_fusion.12
  340.9 4.1 fusion.74
  345.0 4.0 bitcast_add_fusion.12
  350.6 4.1 fusion.74
  354.8 4.0 bitcast_add_fusion.12
  360.4 4.1 fusion.74
  364.5 4.0 bitcast_add_fusion.12
  369.8 9.1 %fusion.41 = bf16[128,8,512]{2,1,0:T(8,128)(2,1)S(1)} fusion(bf16[128,8,4608]{2,1,0:T(8,128)(2,1)} %param.12, bf16[512,4608]{1,0:T(8,128)(2,1)} %all-gather.2.cloned.1.call-done), kind=kOutput, calls=%fused_computation.59 | convolution fusion | flops 4831838208 | bytes 15204352 | tf_op jit(solution)/shard_map/td,ehd->the/dot_general | solution.py:82
  382.5 11.5 %convolution_bitcast_fusion.1 = f32[128,8,4608]{2,0,1:T(8,128)} fusion(bf16[512,8,128]{0,2,1:T(8,128)(2,1)S(1)} %bitcast.231, bf16[512,4608]{1,0:T(8,128)(2,1)} %all-gather.2.cloned.1.call-done), kind=kOutput, calls=%fused_computation.57 | convolution fusion | flops 4831838208 | bytes 24641536 | tf_op jit(solution)/shard_map/the,td->ehd/dot_general | solution.py:56
  394.1 212.0 %while.31 = (s32[]{:T(128)}, f32[512,4,2,128]{0,3,2,1:T(8,128)}, f32[9,2,512,4,128]{2,4,3,1,0:T(8,128)}, bf16[9,2,512,4,128]{4,2,3,1,0:T(8,128)(2,1)}, s32[9]{0:...) while((s32[]{:T(128)}, f32[512,4,2,128]{0,3,2,1:T(8,128)}, ...), condition=%wide.region_5.6_spmd.clone, body=%wide.region_4.5_spmd.clone.sunk | while | flops 2720794624 | bytes 63235308 | solution.py:165
  398.2 3.7 fusion.85
  401.9 5.7 fusion.84
  421.6 3.8 fusion.85
  425.4 5.6 fusion.84
  432.3 4.6 bitcast_add_fusion.13
  445.8 3.7 fusion.85
  449.5 5.6 fusion.84
  456.4 4.0 bitcast_add_fusion.13
  469.4 3.7 fusion.85
  473.0 5.7 fusion.84
  480.0 3.9 bitcast_add_fusion.13
  492.9 3.7 fusion.85
  496.6 5.6 fusion.84
  503.5 3.9 bitcast_add_fusion.13
  516.4 3.7 fusion.85
  520.1 5.7 fusion.84
  527.0 3.9 bitcast_add_fusion.13
  539.8 3.7 fusion.85
  543.5 5.6 fusion.84
  550.4 3.9 bitcast_add_fusion.13
  563.2 3.7 fusion.85
  566.9 5.6 fusion.84
  573.7 4.0 bitcast_add_fusion.13
  586.6 3.7 fusion.85
  590.2 5.6 fusion.84
  597.1 3.9 bitcast_add_fusion.13
  609.8 26.3 %collective-permute-done.8 = f32[2,512,4,128]{1,3,2,0:T(8,128)S(1)} collective-permute-done((f32[2,512,4,128]{1,3,2,0:T(8,128)S(1)}, f32[2,512,4,128]{1,3,2,0:T(8,128)S(1)}, u32[]{:S(2)}, u32[]{:S(2)}) %collective-permute-start.8) | collective-permute-done | bytes 2097184 | tf_op jit(solution)/shard_map/ppermute | solution.py:18
  640.1 26.3 %collective-permute-done.9 = f32[2,512,4,128]{1,3,2,0:T(8,128)S(1)} collective-permute-done((f32[2,512,4,128]{1,3,2,0:T(8,128)S(1)}, f32[2,512,4,128]{1,3,2,0:T(8,128)S(1)}, u32[]{:S(2)}, u32[]{:S(2)}) %collective-permute-start.9) | collective-permute-done | bytes 2097184 | tf_op jit(solution)/shard_map/ppermute | solution.py:18
  670.4 26.3 %collective-permute-done.10 = f32[2,512,4,128]{1,3,2,0:T(8,128)S(1)} collective-permute-done((f32[2,512,4,128]{1,3,2,0:T(8,128)S(1)}, f32[2,512,4,128]{1,3,2,0:T(8,128)S(1)}, u32[]{:S(2)}, u32[]{:S(2)}) %collective-permute-start.10) | collective-permute-done | bytes 2097184 | tf_op jit(solution)/shard_map/ppermute | solution.py:18
  700.8 26.3 %collective-permute-done.11 = f32[2,512,4,128]{1,3,2,0:T(8,128)S(1)} collective-permute-done((f32[2,512,4,128]{1,3,2,0:T(8,128)S(1)}, f32[2,512,4,128]{1,3,2,0:T(8,128)S(1)}, u32[]{:S(2)}, u32[]{:S(2)}) %collective-permute-start.11) | collective-permute-done | bytes 2097184 | tf_op jit(solution)/shard_map/ppermute | solution.py:18
  731.1 26.3 %collective-permute-done.12 = f32[2,512,4,128]{1,3,2,0:T(8,128)S(1)} collective-permute-done((f32[2,512,4,128]{1,3,2,0:T(8,128)S(1)}, f32[2,512,4,128]{1,3,2,0:T(8,128)S(1)}, u32[]{:S(2)}, u32[]{:S(2)}) %collective-permute-start.12) | collective-permute-done | bytes 2097184 | tf_op jit(solution)/shard_map/ppermute | solution.py:18
  761.7 26.1 %collective-permute-done.13 = f32[2,512,4,128]{1,3,2,0:T(8,128)S(1)} collective-permute-done((f32[2,512,4,128]{1,3,2,0:T(8,128)S(1)}, f32[2,512,4,128]{1,3,2,0:T(8,128)S(1)}, u32[]{:S(2)}, u32[]{:S(2)}) %collective-permute-start.13) | collective-permute-done | bytes 2097184 | tf_op jit(solution)/shard_map/ppermute | solution.py:18
  791.7 26.3 %collective-permute-done.14 = f32[2,512,4,128]{1,3,2,0:T(8,128)S(1)} collective-permute-done((f32[2,512,4,128]{1,3,2,0:T(8,128)S(1)}, f32[2,512,4,128]{1,3,2,0:T(8,128)S(1)}, u32[]{:S(2)}, u32[]{:S(2)}) %collective-permute-start.14) | collective-permute-done | bytes 2097184 | tf_op jit(solution)/shard_map/ppermute | solution.py:18
  818.1 3.4 bitcast_add_fusion.3
  834.6 15.4 %collective-permute-done.15 = f32[2,512,4,128]{1,3,2,0:T(8,128)} collective-permute-done((f32[2,512,4,128]{1,3,2,0:T(8,128)}, f32[2,512,4,128]{1,3,2,0:T(8,128)}, u32[]{:S(2)}, u32[]{:S(2)}) %collective-permute-start.15) | collective-permute-done | bytes 2097184 | tf_op jit(solution)/shard_map/ppermute | solution.py:18
  (232 shorter events, 192.6 us)
Async XLA Ops:
  7.2 361.3 %all-gather.2.cloned.1.call-start = ((), (), s32[]{:S(2)}) async-start(), calls=%async_computation.1 | async-start | bytes 7077888 | tf_op jit(solution)/shard_map/all_gather | solution.py:80
  9.9 16.3 %copy-start = (bf16[512,512]{0,1:T(8,128)(2,1)}, bf16[512,512]{0,1:T(8,128)(2,1)S(1)}, u32[]{:S(2)}) copy-start(bf16[512,512]{0,1:T(8,128)(2,1)S(1)} %copy.27) | copy-start | bytes 1572868
  10.4 15.7 %copy-start.7 = (f32[512,64]{0,1:T(8,128)}, f32[512,64]{0,1:T(8,128)S(1)}, u32[]{:S(2)}) copy-start(f32[512,64]{0,1:T(8,128)S(1)} %get-tuple-element.413) | copy-start | bytes 393220
  10.5 16.6 %copy-start.9 = (f32[512,64]{0,1:T(8,128)}, f32[512,64]{0,1:T(8,128)S(1)}, u32[]{:S(2)}) copy-start(f32[512,64]{0,1:T(8,128)S(1)} %get-tuple-element.414) | copy-start | bytes 393220
  10.6 17.2 %copy-start.2 = (bf16[1,512,4,64]{1,3,2,0:T(8,128)(2,1)}, bf16[1,512,4,64]{1,3,2,0:T(8,128)(2,1)S(1)}, u32[]{:S(2)}) copy-start(bf16[1,512,4,64]{1,3,2,0:T(8,128)(2,1)S(1)} %get-tuple-element.412) | copy-start | bytes 786436
  11.7 50.3 %collective-permute-start = (bf16[2,512,4,128]{1,3,2,0:T(8,128)(2,1)}, bf16[2,512,4,128]{1,3,2,0:T(8,128)(2,1)}, u32[]{:S(2)}, u32[]{:S(2)}) collective-permute-start(bf16[2,512,4,128]{1,3,2,0:T(8,128)(2,1)} %pad_maximum_fusion.1), channel_id=1, source_target_pairs={{0,16},{2,18},{4,20},{6,22},{8,24},{10,26},{12,28},{14,30},{1,17},... | collective-permute-start | bytes 3145736 | tf_op jit(solution)/shard_map/ppermute | solution.py:18
  16.9 248.0 %collective-permute-start.7 = (bf16[2,512,4,128]{1,3,2,0:T(8,128)(2,1)}, bf16[2,512,4,128]{1,3,2,0:T(8,128)(2,1)}, u32[]{:S(2)}, u32[]{:S(2)}) collective-permute-start(bf16[2,512,4,128]{1,3,2,0:T(8,128)(2,1)} %pad_maximum_fusion.1), channel_id=1, source_target_pairs={{0,2},{2,4},{4,6},{6,8},{8,10},{10,12},{12,14},{14,16},{16,18},{18... | collective-permute-start | bytes 3145736 | tf_op jit(solution)/shard_map/ppermute | solution.py:18
  18.8 197.4 %collective-permute-start.3 = (bf16[2,512,4,128]{1,3,2,0:T(8,128)(2,1)}, bf16[2,512,4,128]{1,3,2,0:T(8,128)(2,1)}, u32[]{:S(2)}, u32[]{:S(2)}) collective-permute-start(bf16[2,512,4,128]{1,3,2,0:T(8,128)(2,1)} %pad_maximum_fusion.1), channel_id=1, source_target_pairs={{0,10},{2,12},{4,14},{6,16},{8,18},{10,20},{12,22},{14,24},{16,26}... | collective-permute-start | bytes 3145736 | tf_op jit(solution)/shard_map/ppermute | solution.py:18
  20.8 191.0 %collective-permute-start.2 = (bf16[2,512,4,128]{1,3,2,0:T(8,128)(2,1)}, bf16[2,512,4,128]{1,3,2,0:T(8,128)(2,1)}, u32[]{:S(2)}, u32[]{:S(2)}) collective-permute-start(bf16[2,512,4,128]{1,3,2,0:T(8,128)(2,1)} %pad_maximum_fusion.1), channel_id=1, source_target_pairs={{0,12},{2,14},{4,16},{6,18},{8,20},{10,22},{12,24},{14,26},{16,28}... | collective-permute-start | bytes 3145736 | tf_op jit(solution)/shard_map/ppermute | solution.py:18
  22.7 184.9 %collective-permute-start.1 = (bf16[2,512,4,128]{1,3,2,0:T(8,128)(2,1)}, bf16[2,512,4,128]{1,3,2,0:T(8,128)(2,1)}, u32[]{:S(2)}, u32[]{:S(2)}) collective-permute-start(bf16[2,512,4,128]{1,3,2,0:T(8,128)(2,1)} %pad_maximum_fusion.1), channel_id=1, source_target_pairs={{0,14},{2,16},{4,18},{6,20},{8,22},{10,24},{12,26},{14,28},{16,30}... | collective-permute-start | bytes 3145736 | tf_op jit(solution)/shard_map/ppermute | solution.py:18
  24.6 831.2 %reduce-scatter.2.cloned.1.call-start = ((), (), s32[]{:S(2)}) async-start(), calls=%async_computation.2 | async-start | bytes 20054016 | tf_op jit(solution)/shard_map/reduce_scatter | solution.py:57
  27.9 1.0 copy-start.4
  27.9 1.0 copy-start.6
  62.1 168.0 %collective-permute-start.4 = (bf16[2,512,4,128]{1,3,2,0:T(8,128)(2,1)}, bf16[2,512,4,128]{1,3,2,0:T(8,128)(2,1)S(1)}, u32[]{:S(2)}, u32[]{:S(2)}) collective-permute-start(bf16[2,512,4,128]{1,3,2,0:T(8,128)(2,1)} %pad_maximum_fusion.1), channel_id=1, source_target_pairs={{0,8},{2,10},{4,12},{6,14},{8,16},{10,18},{12,20},{14,22},{16,24},... | collective-permute-start | bytes 3145736 | tf_op jit(solution)/shard_map/ppermute | solution.py:18
  207.6 44.9 %collective-permute-start.5 = (bf16[2,512,4,128]{1,3,2,0:T(8,128)(2,1)}, bf16[2,512,4,128]{1,3,2,0:T(8,128)(2,1)S(1)}, u32[]{:S(2)}, u32[]{:S(2)}) collective-permute-start(bf16[2,512,4,128]{1,3,2,0:T(8,128)(2,1)} %pad_maximum_fusion.1), channel_id=1, source_target_pairs={{0,6},{2,8},{4,10},{6,12},{8,14},{10,16},{12,18},{14,20},{16,22},{... | collective-permute-start | bytes 3145736 | tf_op jit(solution)/shard_map/ppermute | solution.py:18
  211.8 52.1 %collective-permute-start.6 = (bf16[2,512,4,128]{1,3,2,0:T(8,128)(2,1)}, bf16[2,512,4,128]{1,3,2,0:T(8,128)(2,1)S(1)}, u32[]{:S(2)}, u32[]{:S(2)}) collective-permute-start(bf16[2,512,4,128]{1,3,2,0:T(8,128)(2,1)} %pad_maximum_fusion.1), channel_id=1, source_target_pairs={{0,4},{2,6},{4,8},{6,10},{8,12},{10,14},{12,16},{14,18},{16,20},{1... | collective-permute-start | bytes 3145736 | tf_op jit(solution)/shard_map/ppermute | solution.py:18
  218.5 48.7 %copy-start.1 = (bf16[512,512]{0,1:T(8,128)(2,1)S(1)}, bf16[512,512]{0,1:T(8,128)(2,1)}, u32[]{:S(2)}) copy-start(bf16[512,512]{0,1:T(8,128)(2,1)} %copy-done) | copy-start | bytes 1572868
  218.5 48.7 %copy-start.3 = (bf16[1,512,4,64]{1,3,2,0:T(8,128)(2,1)S(1)}, bf16[1,512,4,64]{1,3,2,0:T(8,128)(2,1)}, u32[]{:S(2)}) copy-start(bf16[1,512,4,64]{1,3,2,0:T(8,128)(2,1)} %copy-done.2) | copy-start | bytes 786436
  268.2 12.8 %copy-start.11 = (f32[512,4,2,128]{0,3,2,1:T(8,128)S(1)}, f32[512,4,2,128]{0,3,2,1:T(8,128)}, u32[]{:S(2)}) copy-start(f32[512,4,2,128]{0,3,2,1:T(8,128)} %custom-call.1) | copy-start | bytes 6291460
  368.4 1.3 copy-start.12
  607.9 28.3 %collective-permute-start.8 = (f32[2,512,4,128]{1,3,2,0:T(8,128)S(1)}, f32[2,512,4,128]{1,3,2,0:T(8,128)S(1)}, u32[]{:S(2)}, u32[]{:S(2)}) collective-permute-start(f32[2,512,4,128]{1,3,2,0:T(8,128)S(1)} %slice_bitcast_fusion), channel_id=1, source_target_pairs={{2,0},{4,2},{6,4},{8,6},{10,8},{12,10},{14,12},{16,14},{18,16},{20... | collective-permute-start | bytes 6291464 | tf_op jit(solution)/shard_map/ppermute | solution.py:18
  638.2 28.3 %collective-permute-start.9 = (f32[2,512,4,128]{1,3,2,0:T(8,128)S(1)}, f32[2,512,4,128]{1,3,2,0:T(8,128)S(1)}, u32[]{:S(2)}, u32[]{:S(2)}) collective-permute-start(f32[2,512,4,128]{1,3,2,0:T(8,128)S(1)} %bitcast_add_fusion.9), channel_id=1, source_target_pairs={{2,0},{4,2},{6,4},{8,6},{10,8},{12,10},{14,12},{16,14},{18,16},{20... | collective-permute-start | bytes 6291464 | tf_op jit(solution)/shard_map/ppermute | solution.py:18
  668.5 28.3 %collective-permute-start.10 = (f32[2,512,4,128]{1,3,2,0:T(8,128)S(1)}, f32[2,512,4,128]{1,3,2,0:T(8,128)S(1)}, u32[]{:S(2)}, u32[]{:S(2)}) collective-permute-start(f32[2,512,4,128]{1,3,2,0:T(8,128)S(1)} %bitcast_add_fusion.8), channel_id=1, source_target_pairs={{2,0},{4,2},{6,4},{8,6},{10,8},{12,10},{14,12},{16,14},{18,16},{20... | collective-permute-start | bytes 6291464 | tf_op jit(solution)/shard_map/ppermute | solution.py:18
  698.8 28.3 %collective-permute-start.11 = (f32[2,512,4,128]{1,3,2,0:T(8,128)S(1)}, f32[2,512,4,128]{1,3,2,0:T(8,128)S(1)}, u32[]{:S(2)}, u32[]{:S(2)}) collective-permute-start(f32[2,512,4,128]{1,3,2,0:T(8,128)S(1)} %bitcast_add_fusion.7), channel_id=1, source_target_pairs={{2,0},{4,2},{6,4},{8,6},{10,8},{12,10},{14,12},{16,14},{18,16},{20... | collective-permute-start | bytes 6291464 | tf_op jit(solution)/shard_map/ppermute | solution.py:18
  729.2 28.3 %collective-permute-start.12 = (f32[2,512,4,128]{1,3,2,0:T(8,128)S(1)}, f32[2,512,4,128]{1,3,2,0:T(8,128)S(1)}, u32[]{:S(2)}, u32[]{:S(2)}) collective-permute-start(f32[2,512,4,128]{1,3,2,0:T(8,128)S(1)} %bitcast_add_fusion.6), channel_id=1, source_target_pairs={{2,0},{4,2},{6,4},{8,6},{10,8},{12,10},{14,12},{16,14},{18,16},{20... | collective-permute-start | bytes 6291464 | tf_op jit(solution)/shard_map/ppermute | solution.py:18
  759.5 28.3 %collective-permute-start.13 = (f32[2,512,4,128]{1,3,2,0:T(8,128)S(1)}, f32[2,512,4,128]{1,3,2,0:T(8,128)S(1)}, u32[]{:S(2)}, u32[]{:S(2)}) collective-permute-start(f32[2,512,4,128]{1,3,2,0:T(8,128)S(1)} %bitcast_add_fusion.5), channel_id=1, source_target_pairs={{2,0},{4,2},{6,4},{8,6},{10,8},{12,10},{14,12},{16,14},{18,16},{20... | collective-permute-start | bytes 6291464 | tf_op jit(solution)/shard_map/ppermute | solution.py:18
  789.8 28.3 %collective-permute-start.14 = (f32[2,512,4,128]{1,3,2,0:T(8,128)S(1)}, f32[2,512,4,128]{1,3,2,0:T(8,128)S(1)}, u32[]{:S(2)}, u32[]{:S(2)}) collective-permute-start(f32[2,512,4,128]{1,3,2,0:T(8,128)S(1)} %bitcast_add_fusion.4), channel_id=1, source_target_pairs={{2,0},{4,2},{6,4},{8,6},{10,8},{12,10},{14,12},{16,14},{18,16},{20... | collective-permute-start | bytes 6291464 | tf_op jit(solution)/shard_map/ppermute | solution.py:18
  821.5 28.6 %collective-permute-start.15 = (f32[2,512,4,128]{1,3,2,0:T(8,128)}, f32[2,512,4,128]{1,3,2,0:T(8,128)}, u32[]{:S(2)}, u32[]{:S(2)}) collective-permute-start(f32[2,512,4,128]{1,3,2,0:T(8,128)} %bitcast_add_fusion.3), channel_id=1, source_target_pairs={{2,0},{4,2},{6,4},{8,6},{10,8},{12,10},{14,12},{16,14},{18,16},{20... | collective-permute-start | bytes 6291464 | tf_op jit(solution)/shard_map/ppermute | solution.py:18
  826.2 4.0 copy-start.5
  852.8 1.5 copy-start.8
  852.8 1.5 copy-start.10
Sparse Core Ops, SparseCore 0:
  24.8 63.5 all-gather.1
  394.2 193.3 reduce-scatter.1
where the time goes:
time: 869 us; the launch traced here: 866 us
  waiting for transfers between devices  415 us (48%)
  matrix products  244 us (28%)
  local copies, waits for them, and re-layouts  95.3 us (11%)
  other arithmetic  48.9 us (6%)
  starting transfers between devices  34.5 us (4%)
  between operations  14.5 us (2%)
  loops' own time  13.1 us (2%)
    ppermute x16, waiting for transfers between devices, passed_along(): return lax.ppermute(block, axis, route)  415 us
    dot_general x18, matrix products, tile_setup(): jnp.einsum('qfwy,vfy->fwqv', query_rotated, key_panel[0], preferred_eleme...  57.4 us
    dot_general x9, matrix products, backward_tile(): jnp.einsum('qfwy,vfy->fwqv', output_gradient, key_panel[1], preferred_ele...  50.7 us
    unnamed x45, local copies, waits for them, and re-layouts  45.1 us
    dot_general x9, matrix products, forward_tile(): jnp.einsum('fpxe,efv->xfpv', exponent_score.astype(jnp.bfloat16), key_pan...  35.6 us
    dot_general x9, matrix products, backward_tile(): jnp.einsum('fpxe,efv->xfpv', score_gradient, key_panel[0], preferred_elem...  35.4 us
    ppermute x16, starting transfers between devices, passed_along(): return lax.ppermute(block, axis, route)  34.4 us
    dot_general x9, matrix products, backward_tile(): jnp.einsum('vcfh,fvcx->hvx', softmax_probability.astype(jnp.bfloat16), ou...  33.1 us
  transfers between devices with their start and end apart: 18, of which 13 were waited for; matrix products, arithmetic and copies ran while one was open for 41% of the time, Pallas kernels for 0%

commit v1 on v0

v1 whole, which is shorter than its diff:
```python
import functools

import jax
import jax.numpy as jnp
from jax import lax
from jax.experimental import pallas as pl
from jax.experimental.pallas import tpu as pltpu
from jax.sharding import PartitionSpec as P

SPAN = 8
SOFT_CAP = 50.0
QUERY_MULTIPLIER = 144.0 ** (-0.5)
ROPE_BASE = 10000.0
LOG2E = 1.4426950408889634
F32, BF16 = jnp.float32, jnp.bfloat16
NT = (((1,), (1,)), ((), ()))
NN = (((1,), (0,)), ((), ()))


def dot(a, b, dims=NN):
    return lax.dot_general(a, b, dims, preferred_element_type=F32)


def rotary_tables(positions, width):
    half_width = width // 2
    frequency = ROPE_BASE ** (-(jnp.arange(half_width, dtype=jnp.float32) * 2.0) / width)
    angles = positions.astype(jnp.float32)[:, None] * frequency[None, :]
    return (jnp.cos(angles)[:, None, :], jnp.sin(angles)[:, None, :])


def rotate(values_in, cosine, sine):
    half = values_in.shape[-1] // 2
    a, b = values_in[..., :half], values_in[..., half:]
    return jnp.concatenate([a * cosine - b * sine, b * cosine + a * sine], axis=-1)


def tanh_of(scores):
    return jnp.tanh(scores * (QUERY_MULTIPLIER / SOFT_CAP))


def exp_of(th):
    return jnp.exp2(th * (SOFT_CAP * LOG2E))


def fwd_kernel(tok, hd, heads, start_ref, q_ref, kv_ref, attn_ref, linv_ref, acc_ref):
    i = pl.program_id(0)
    j0 = start_ref[0]
    row = lax.broadcasted_iota(jnp.int32, (tok, tok), 0)
    col = lax.broadcasted_iota(jnp.int32, (tok, tok), 1)

    def tile(j, mask, first):
        rows = pl.ds(pl.multiple_of(j * tok, tok), tok)
        k = kv_ref[rows, 0:hd]
        vx = kv_ref[rows, hd : 3 * hd]
        for h in range(heads):
            s = dot(q_ref[:, h * hd : (h + 1) * hd], k, NT)
            e = exp_of(tanh_of(s))
            if mask is not None:
                e = jnp.where(mask, e, 0.0)
            part = dot(e.astype(BF16), vx)
            if first:
                acc_ref[h] = part
            else:
                acc_ref[h] += part

    tile(i + SPAN, row >= col, True)

    def mid(j, carry):
        tile(j, None, False)
        return carry

    lax.fori_loop(jnp.maximum(i + 1, j0), i + SPAN, mid, 0)

    @pl.when(i >= j0)
    def _():
        tile(i, row < col, False)

    for h in range(heads):
        total = acc_ref[h, :, hd : 2 * hd]
        inv = 1.0 / total
        cols = slice(h * hd, (h + 1) * hd)
        attn_ref[:, cols] = (acc_ref[h, :, 0:hd] * inv).astype(BF16)
        linv_ref[:, cols] = inv


def bwd_kernel(
    tok, hd, heads, start_ref, q_ref, attn_ref, linv_ref, do_ref, kv_ref, kt_ref,
    gq_ref, gkv_ref, qs_ref, dos_ref, dox_ref, dqt_ref,
):
    i = pl.program_id(0)
    j0 = start_ref[0]
    key = lax.broadcasted_iota(jnp.int32, (tok, tok), 0)
    qry = lax.broadcasted_iota(jnp.int32, (tok, tok), 1)

    @pl.when(i == 0)
    def _():
        gkv_ref[...] = jnp.zeros_like(gkv_ref)

    lane = lax.broadcasted_iota(jnp.int32, (tok, hd), 1)
    for h in range(heads):
        cols = slice(h * hd, (h + 1) * hd)
        inv = linv_ref[:, cols]
        do = do_ref[:, cols]
        dof = do.astype(F32)
        qs_ref[:, cols] = (q_ref[:, cols].astype(F32) * (inv * QUERY_MULTIPLIER)).astype(BF16)
        dos_ref[:, cols] = (dof * inv).astype(BF16)
        delta = jnp.sum(dof * attn_ref[:, cols].astype(F32), axis=-1, keepdims=True)
        delta = jnp.broadcast_to(-delta, (tok, hd))
        hi = delta.astype(BF16).astype(F32)
        lo = (delta - hi).astype(BF16).astype(F32)
        lo2 = delta - hi - lo
        packed = jnp.where(
            lane == 0, hi, jnp.where(lane == 1, lo, jnp.where(lane == 2, lo2, 0.0))
        )
        dox_ref[h, :, 0:hd] = do
        dox_ref[h, :, hd : 2 * hd] = packed.astype(BF16)

    def tile(j, mask, first):
        rows = pl.ds(pl.multiple_of(j * tok, tok), tok)
        k = kv_ref[rows, 0:hd]
        vx = kv_ref[rows, hd : 3 * hd]
        kt = kt_ref[:, rows]
        gk = None
        for h in range(heads):
            cols = slice(h * hd, (h + 1) * hd)
            th = tanh_of(dot(k, q_ref[:, cols], NT))
            e = exp_of(th)
            if mask is not None:
                e = jnp.where(mask, e, 0.0)
            dp = dot(vx, dox_ref[h], NT)
            ds = (e * (1.0 - th * th) * dp).astype(BF16)
            part_v = dot(e.astype(BF16), dos_ref[:, cols])
            part_k = dot(ds, qs_ref[:, cols])
            part_q = dot(kt, ds)
            if first:
                dqt_ref[h] = part_q
            else:
                dqt_ref[h] += part_q
            gk = part_k if gk is None else gk + part_k
            gv = part_v if h == 0 else gv + part_v
        gkv_ref[rows, 0:hd] += gk
        gkv_ref[rows, hd : 2 * hd] += gv

    tile(i + SPAN, qry >= key, True)

    def mid(j, carry):
        tile(j, None, False)
        return carry

    lax.fori_loop(jnp.maximum(i + 1, j0), i + SPAN, mid, 0)

    @pl.when(i >= j0)
    def _():
        tile(i, qry < key, False)

    for h in range(heads):
        cols = slice(h * hd, (h + 1) * hd)
        gq = dqt_ref[h].T * (linv_ref[:, cols] * QUERY_MULTIPLIER)
        gq_ref[:, cols] = gq.astype(BF16)


def local(queries, keys, values, out_weight, cotangent):
    tok = queries.shape[0]
    hd = out_weight.shape[0]
    nq = queries.shape[1] // hd
    group = keys.shape[1] // hd
    heads = nq // group
    n_ctx = lax.axis_size("ctx")
    n_head = lax.axis_size("head")
    hops = SPAN // group
    me = lax.axis_index("ctx")
    rank = me % group
    chunk = group * tok

    def exchange(payload):
        out = jnp.zeros_like(payload)
        own = lax.dynamic_index_in_dim(payload, rank, 0)
        out = lax.dynamic_update_slice_in_dim(out, own, rank, 0)
        for d in range(1, group):
            piece = lax.dynamic_index_in_dim(payload, (rank + d) % group, 0)
            route = [(s, s - s % group + (s % group + d) % group) for s in range(n_ctx)]
            got = lax.ppermute(piece, "ctx", route)
            out = lax.dynamic_update_slice_in_dim(out, got, (rank - d) % group, 0)
        return out

    def shift(block, by):
        route = [(s, s + by) for s in range(n_ctx) if 0 <= s + by < n_ctx]
        return lax.ppermute(block, "ctx", route)

    if n_head == 2:
        other = lax.ppermute(cotangent, "head", [(0, 1), (1, 0)])
        first = lax.axis_index("head") == 0
        full_grad = jnp.concatenate(
            [jnp.where(first, cotangent, other), jnp.where(first, other, cotangent)], axis=0
        )
    else:
        full_grad = lax.all_gather(cotangent, "head", axis=0, tiled=True)

    positions = me * tok + jnp.arange(tok, dtype=jnp.int32)
    cosine, sine = rotary_tables(positions, hd)
    qr = rotate(queries.reshape(tok, nq, hd).astype(F32), cosine, sine).astype(BF16)
    kr = rotate(keys.reshape(tok, group, hd).astype(F32), cosine, sine).astype(BF16)
    payload = jnp.concatenate(
        [qr.reshape(tok, group, heads * hd), kr, values.reshape(tok, group, hd)], axis=-1
    ).transpose(1, 0, 2)
    mine = exchange(payload).reshape(chunk, (heads + 2) * hd)
    q_own = mine[:, : heads * hd]
    window = [mine[:, heads * hd :]]
    for _ in range(hops):
        window.insert(0, shift(window[0], group))
    kv = jnp.concatenate(window, axis=0)
    kv_rows = kv.shape[0]
    kv = jnp.concatenate([kv, jnp.ones((kv_rows, hd), BF16)], axis=1)
    start = jnp.maximum(0, SPAN - (me // group) * group).astype(jnp.int32).reshape(1)

    width = heads * hd
    smem = pl.BlockSpec(memory_space=pltpu.SMEM)
    by_query = pl.BlockSpec((tok, width), lambda i: (i, 0))
    kv_spec = pl.BlockSpec((kv_rows, 3 * hd), lambda i: (0, 0))
    pairs = chunk * heads * SPAN * tok
    attn, linv = pl.pallas_call(
        functools.partial(fwd_kernel, tok, hd, heads),
        grid=(group,),
        out_shape=(
            jax.ShapeDtypeStruct((chunk, width), BF16),
            jax.ShapeDtypeStruct((chunk, width), F32),
        ),
        in_specs=[smem, by_query, kv_spec],
        out_specs=(by_query, by_query),
        scratch_shapes=[pltpu.VMEM((heads, tok, 2 * hd), F32)],
        compiler_params=pltpu.CompilerParams(vmem_limit_bytes=56 * 2**20),
        cost_estimate=pl.CostEstimate(
            flops=8 * pairs * hd, bytes_accessed=8 * 2**20, transcendentals=2 * pairs
        ),
        name="attend",
    )(start, q_own, kv)

    dout = jnp.einsum("td,ehd->the", full_grad, out_weight, preferred_element_type=F32)
    dout = dout.astype(BF16).reshape(tok, group, width).transpose(1, 0, 2)
    dout_own = exchange(dout).reshape(chunk, width)

    attn_tok = exchange(attn.reshape(group, tok, width)).transpose(1, 0, 2).reshape(tok, nq, hd)
    term = jnp.einsum("the,td->ehd", attn_tok, full_grad, preferred_element_type=F32)
    term = term.astype(BF16).reshape(n_ctx, hd // n_ctx, nq, full_grad.shape[1])
    bit = 1
    while bit < n_ctx:
        term = term.reshape(term.shape[0] // 2, 2, *term.shape[1:])
        mine_bit = (me // bit) % 2
        keep = lax.dynamic_index_in_dim(term, mine_bit, 1, keepdims=False)
        send = lax.dynamic_index_in_dim(term, 1 - mine_bit, 1, keepdims=False)
        got = lax.ppermute(send, "ctx", [(s, s ^ bit) for s in range(n_ctx)])
        total = keep.astype(F32) + got.astype(F32)
        bit *= 2
        term = total.astype(BF16) if bit < n_ctx else total
    weight_grad = term[0]

    kt = kv[:, 0:hd].T
    gq, gkv = pl.pallas_call(
        functools.partial(bwd_kernel, tok, hd, heads),
        grid=(group,),
        out_shape=(
            jax.ShapeDtypeStruct((chunk, width), BF16),
            jax.ShapeDtypeStruct((kv_rows, 2 * hd), F32),
        ),
        in_specs=[
            smem, by_query, by_query, by_query, by_query, kv_spec,
            pl.BlockSpec((hd, kv_rows), lambda i: (0, 0)),
        ],
        out_specs=(by_query, pl.BlockSpec((kv_rows, 2 * hd), lambda i: (0, 0))),
        scratch_shapes=[
            pltpu.VMEM((tok, width), BF16),
            pltpu.VMEM((tok, width), BF16),
            pltpu.VMEM((heads, tok, 2 * hd), BF16),
            pltpu.VMEM((heads, hd, tok), F32),
        ],
        compiler_params=pltpu.CompilerParams(vmem_limit_bytes=56 * 2**20),
        cost_estimate=pl.CostEstimate(
            flops=20 * pairs * hd, bytes_accessed=20 * 2**20, transcendentals=2 * pairs
        ),
        name="attend_grad",
    )(start, q_own, attn, linv, dout_own, kv, kt)

    parts = gkv.reshape(hops + 1, chunk, 2 * hd)
    running = parts[0]
    for step in range(hops):
        running = shift(running.astype(BF16), -group).astype(F32) + parts[step + 1]
    gq_tok = exchange(gq.reshape(group, tok, width)).transpose(1, 0, 2)
    gkv_tok = exchange(running.astype(BF16).reshape(group, tok, 2 * hd)).transpose(1, 0, 2)
    query_grad = rotate(gq_tok.reshape(tok, nq, hd).astype(F32), cosine, -sine)
    key_grad = rotate(gkv_tok[..., :hd].astype(F32), cosine, -sine)
    value_grad = gkv_tok[..., hd:].astype(F32)
    return (
        query_grad.reshape(tok, nq * hd),
        key_grad.reshape(tok, group * hd),
        value_grad.reshape(tok, group * hd),
        weight_grad,
    )


def solution(mesh):
    placed = (
        P("ctx", "head"),
        P("ctx", "head"),
        P("ctx", "head"),
        P(None, "head", None),
        P(("ctx", "head"), None),
    )
    return jax.shard_map(
        local,
        mesh=mesh,
        in_specs=placed,
        out_specs=(P("ctx", "head"), P("ctx", "head"), P("ctx", "head"), P("ctx", "head", None)),
        check_vma=False,
    )
```

time: 869 us -> 444 us (0.51)
  the two profiles are of different devices: /device:TPU:15 before, /device:TPU:0 now
where the time goes in v1:
time: 444 us; the launch traced here: 437 us
  waiting for transfers between devices  185 us (42%)
  local copies, waits for them, and re-layouts  128 us (29%)
  Pallas kernels  38.2 us (9%)
  starting transfers between devices  33.6 us (8%)
  other arithmetic  29.4 us (7%)
  matrix products  20.6 us (5%)
    ppermute x4, waiting for transfers between devices, shift(): return lax.ppermute(block, 'ctx', route)  138 us
    dynamic_update_slice x16, local copies, waits for them, and re-layouts, exchange(): out = lax.dynamic_update_slice_in_dim(out, got, (rank - d) % group, 0)  40.5 us
    ppermute x4, waiting for transfers between devices, local(): got = lax.ppermute(send, 'ctx', [(s, s ^ bit) for s in range(n_ctx)])  38.2 us
    unnamed x75, local copies, waits for them, and re-layouts  32.7 us
    pallas_call x1, Pallas kernels, local(): pl.pallas_call(functools.partial(bwd_kernel, tok, hd, heads), grid=(group...  26.2 us
    ppermute x15, starting transfers between devices, exchange(): got = lax.ppermute(piece, 'ctx', route)  13.1 us
    pallas_call x1, Pallas kernels, local(): pl.pallas_call(functools.partial(fwd_kernel, tok, hd, heads), grid=(group...  12 us
    dynamic_update_slice x5, local copies, waits for them, and re-layouts, exchange(): out = lax.dynamic_update_slice_in_dim(out, own, rank, 0)  11.5 us
  transfers between devices with their start and end apart: 24, of which 7 were waited for; matrix products, arithmetic and copies ran while one was open for 37% of the time, Pallas kernels for 6%

profile of v1, /device:TPU:0, one launch (start us, length us, event | category | flops | bytes accessed | tf_op | source)
XLA Modules:
  0.0 437.4 jit_solution(9621167393454065274)
XLA Ops:
  0.6 3.0 collective-permute-start.5
  3.7 2.1 copy.48
  7.1 1.5 copy.46
  12.4 2.1 copy.51
  15.5 1.5 collective-permute-start.1
  18.0 1.5 collective-permute-start.2
  20.9 8.8 %dynamic_update_slice.60 = bf16[4,512,512]{1,0,2:T(4,128)(2,1)S(1)} dynamic-update-slice(bf16[4,512,512]{1,0,2:T(4,128)(2,1)S(1)} %broadcast_in_dim.2, bf16[1,512,512]{1,0,2:T(2,128)(2,1)S(1)} %copy.50, s32[]{:T(128)S(6)} %select_n.205, s32[]{:T(128)} %constant.236.clone.1, s32[]{:T(128)} %constant.236.clone.1) | dynamic-update-slice | bytes 1048580 | tf_op jit(solution)/shard_map/dynamic_update_slice | solution.py:178
  29.7 2.4 copy.52
  32.1 8.8 %dynamic_update_slice.61 = bf16[4,512,512]{1,0,2:T(4,128)(2,1)S(1)} dynamic-update-slice(bf16[4,512,512]{1,0,2:T(4,128)(2,1)S(1)} %dynamic_update_slice.60, bf16[1,512,512]{1,0,2:T(2,128)(2,1)S(1)} %copy.52, s32[]{:T(128)S(6)} %select_n.209, s32[]{:T(128)} %constant.236.clone.1, s32[]{:T(128)} %constant.236.clone.1) | dynamic-update-slice | bytes 1048580 | tf_op jit(solution)/shard_map/dynamic_update_slice | solution.py:183
  40.9 2.4 copy.54
  43.3 8.8 %dynamic_update_slice.62 = bf16[4,512,512]{1,0,2:T(4,128)(2,1)S(1)} dynamic-update-slice(bf16[4,512,512]{1,0,2:T(4,128)(2,1)S(1)} %dynamic_update_slice.61, bf16[1,512,512]{1,0,2:T(2,128)(2,1)S(1)} %copy.54, s32[]{:T(128)S(6)} %select_n.213, s32[]{:T(128)} %constant.236.clone.1, s32[]{:T(128)} %constant.236.clone.1) | dynamic-update-slice | bytes 1048580 | tf_op jit(solution)/shard_map/dynamic_update_slice | solution.py:183
  52.1 2.4 copy.56
  54.6 8.8 %dynamic_update_slice.63 = bf16[4,512,512]{1,0,2:T(4,128)(2,1)S(1)} dynamic-update-slice(bf16[4,512,512]{1,0,2:T(4,128)(2,1)S(1)} %dynamic_update_slice.62, bf16[1,512,512]{1,0,2:T(2,128)(2,1)S(1)} %copy.56, s32[]{:T(128)S(6)} %select_n.217, s32[]{:T(128)} %constant.236.clone.1, s32[]{:T(128)} %constant.236.clone.1) | dynamic-update-slice | bytes 1048580 | tf_op jit(solution)/shard_map/dynamic_update_slice | solution.py:183
  64.1 3.5 collective-permute-start.3
  67.8 1.3 copy.61.q_ref
  69.1 20.2 %collective-permute-done.3 = bf16[2048,256]{0,1:T(8,128)(2,1)S(1)} collective-permute-done((bf16[2048,256]{0,1:T(8,128)(2,1)S(1)}, bf16[2048,256]{0,1:T(8,128)(2,1)S(1)}, u32[]{:S(2)}, u32[]{:S(2)}) %collective-permute-start.3) | collective-permute-done | bytes 1048608 | tf_op jit(solution)/shard_map/ppermute | solution.py:188
  89.2 4.6 %collective-permute-start.4 = (bf16[2048,256]{0,1:T(8,128)(2,1)S(1)}, bf16[2048,256]{0,1:T(8,128)(2,1)S(1)}, u32[]{:S(2)}, u32[]{:S(2)}) collective-permute-start(bf16[2048,256]{0,1:T(8,128)(2,1)S(1)} %collective-permute-done.3), channel_id=1, source_target_pairs={{0,8},{2,10},{4,12},{6,14},{8,16},{10,18},{12,20},{14,22},{16,24},... | collective-permute-start | bytes 3145736 | tf_op jit(solution)/shard_map/ppermute | solution.py:188
  93.9 2.7 broadcast_select_fusion.1
  96.6 11.4 %fusion.7 = bf16[512,128,8]{0,1,2:T(8,128)(2,1)} fusion(bf16[128,8,4608]{2,1,0:T(8,128)(2,1)} %param.8, bf16[256,4608]{1,0:T(8,128)(2,1)S(1)} %get-tuple-element.23, bf16[256,4608]{1,0:T(8,128)(2,1)S(1)} %get-tuple-element.22), kind=kOutput, calls=%fused_computation.23 | convolution fusion | flops 4841799680 | bytes 15204352 | tf_op jit(solution)/shard_map/td,ehd->the/dot_general | solution.py:238
  108.1 6.2 %collective-permute-done.4 = bf16[2048,256]{0,1:T(8,128)(2,1)S(1)} collective-permute-done((bf16[2048,256]{0,1:T(8,128)(2,1)S(1)}, bf16[2048,256]{0,1:T(8,128)(2,1)S(1)}, u32[]{:S(2)}, u32[]{:S(2)}) %collective-permute-start.4) | collective-permute-done | bytes 1048608 | tf_op jit(solution)/shard_map/ppermute | solution.py:188
  114.6 3.3 copy.95
  117.9 4.4 %concatenate.28.clone.kv_ref = bf16[6144,384]{1,0:T(8,128)(2,1)} pad(bf16[6144,256]{1,0:T(8,128)(2,1)} %copy.95, bf16[]{:T(256)} %constant.247.clone.1), padding=0_0x0_128 | pad | bytes 7864322 | tf_op jit(solution)/shard_map/concatenate | solution.py:213
  122.3 12.0 %attend.1 = (bf16[2048,256]{1,0:T(8,128)(2,1)}, f32[2048,256]{1,0:T(8,128)}) custom-call(s32[1]{0:T(128)} %bitcast.start_ref, bf16[2048,256]{1,0:T(8,128)(2,1)} %copy.61.q_ref, bf16[6144,384]{1,0:T(8,128)(2,1)} %concatenate.28.clone.kv_ref), custom_call_target="tpu_custom_call" | custom-call | flops 17179869184 | bytes 8388608 | tf_op jit(solution)/shard_map/attend/pallas_call | solution.py:221
  134.3 2.2 constant_dynamic-slice_fusion.2
  139.1 2.2 collective-permute-start.18
  143.2 1.7 collective-permute-start.7
  146.1 1.8 copy.93
  150.6 9.0 %collective-permute-done.19 = bf16[1,512,256]{1,2,0:T(8,128)(2,1)S(1)} collective-permute-done((bf16[1,512,256]{1,2,0:T(8,128)(2,1)}, bf16[1,512,256]{1,2,0:T(8,128)(2,1)S(1)}, u32[]{:S(2)}, u32[]{:S(2)}) %collective-permute-start.19) | collective-permute-done | bytes 262176 | tf_op jit(solution)/shard_map/ppermute | solution.py:182
  159.7 9.1 %fusion.5 = f32[4608,1024]{0,1} fusion(bf16[512,1024]{0,1:T(8,128)(2,1)S(1)} %bitcast.103, bf16[256,4608]{1,0:T(8,128)(2,1)S(1)} %copy-done.12, bf16[256,4608]{1,0:T(8,128)(2,1)S(1)} %copy-done.10), kind=kOutput, calls=%fused_computation.11 | convolution fusion | flops 4841275392 | bytes 24641536
  168.8 6.9 %convert_element_type.123 = bf16[4608,8,128]{0,2,1:T(8,128)(2,1)S(1)} convert(f32[4608,8,128]{0,2,1:T(8,128)} %bitcast.81) | non-fusion elementwise | flops 4718592 | bytes 28311552 | tf_op jit(solution)/shard_map/convert_element_type | solution.py:244
  175.8 4.3 constant_dynamic-slice_fusion.1
  180.1 7.2 %copy.105 = bf16[8,1,8,8,4608]{4,3,2,0,1:T(8,128)(2,1)} copy(bf16[8,1,8,8,4608]{4,2,1,0,3:T(8,128)(2,1)} %get-tuple-element.21) | data formatting | bytes 9437184 | tf_op jit(solution)/shard_map/jit(dynamic_index_in_dim)/dynamic_slice | solution.py:250
  188.5 1.7 constant_dynamic-update-slice_fusion.14
  190.9 1.7 constant_dynamic-update-slice_fusion.12
  192.6 2.3 copy.60
  194.9 26.2 %attend_grad.1 = (bf16[2048,256]{1,0:T(8,128)(2,1)}, f32[6144,256]{1,0:T(8,128)}) custom-call(s32[1]{0:T(128)} %bitcast.start_ref, bf16[2048,256]{1,0:T(8,128)(2,1)} %copy.61.q_ref, bf16[2048,256]{1,0:T(8,128)(2,1)} %get-tuple-element.8.attn_ref, f32[2048,256]{1,0:T(8,128)} %get-tuple-element.9.linv_ref, bf16[2048,256]{1,0:T(8,128)(2,1)} %bitcast.102, ...), custom_call_target="tpu_custom_call" | custom-call | flops 42949672960 | bytes 20971520 | tf_op jit(solution)/shard_map/attend_grad/pallas_call | solution.py:258
  221.1 1.8 slice.103
  222.9 1.4 collective-permute-start.12
  224.4 5.3 %fusion = bf16[8,8,8,4608]{3,2,1,0:T(8,128)(2,1)S(1)} fusion(bf16[8,8,8,4608]{3,2,1,0:T(8,128)(2,1)} %collective-permute-done.20, bf16[8,1,8,8,4608]{4,2,1,0,3:T(8,128)(2,1)S(1)} %bitcast.83), kind=kLoop, calls=%fused_computation.1 | loop fusion | flops 9437184 | bytes 14155776 | tf_op jit(solution)/shard_map/convert_element_type | solution.py:254
  230.0 2.0 copy-done.2
  231.9 2.2 collective-permute-start.21
  234.1 60.0 %collective-permute-done.12 = bf16[2048,256]{1,0:T(8,128)(2,1)} collective-permute-done((bf16[2048,256]{1,0:T(8,128)(2,1)S(1)}, bf16[2048,256]{1,0:T(8,128)(2,1)}, u32[]{:S(2)}, u32[]{:S(2)}) %collective-permute-start.12) | collective-permute-done | bytes 1048608 | tf_op jit(solution)/shard_map/ppermute | solution.py:188
  294.1 1.6 add_convert_fusion.1
  295.7 1.4 collective-permute-start.13
  297.1 51.7 %collective-permute-done.13 = bf16[2048,256]{1,0:T(8,128)(2,1)S(1)} collective-permute-done((bf16[2048,256]{1,0:T(8,128)(2,1)S(1)}, bf16[2048,256]{1,0:T(8,128)(2,1)S(1)}, u32[]{:S(2)}, u32[]{:S(2)}) %collective-permute-start.13) | collective-permute-done | bytes 1048608 | tf_op jit(solution)/shard_map/ppermute | solution.py:188
  349.1 1.3 constant_dynamic-slice_fusion.6
  350.5 1.9 copy.83
  352.3 1.8 copy.82
  354.2 1.8 copy.84
  357.2 1.8 copy.85
  359.0 1.5 collective-permute-start.11
  363.2 1.8 copy.88
  365.1 1.8 copy.89
  369.8 1.8 collective-permute-start.16
  372.6 2.9 fusion.3
  376.6 1.7 collective-permute-start.22
  379.9 1.6 pad_maximum_fusion.5
  381.5 3.0 copy.77
  388.4 16.0 %collective-permute-done.22 = bf16[2,8,8,4608]{3,2,1,0:T(8,128)(2,1)} collective-permute-done((bf16[2,8,8,4608]{3,2,1,0:T(8,128)(2,1)}, bf16[2,8,8,4608]{3,2,1,0:T(8,128)(2,1)}, u32[]{:S(2)}, u32[]{:S(2)}) %collective-permute-start.22) | collective-permute-done | bytes 1179680 | tf_op jit(solution)/shard_map/ppermute | solution.py:251
  404.4 1.5 fusion.6
  406.8 2.6 collective-permute-start.23
  411.2 1.3 copy.79
  412.5 22.2 %collective-permute-done.23 = bf16[1,8,8,4608]{3,2,1,0:T(8,128)(2,1)} collective-permute-done((bf16[1,8,8,4608]{3,2,1,0:T(8,128)(2,1)}, bf16[1,8,8,4608]{3,2,1,0:T(8,128)(2,1)}, u32[]{:S(2)}, u32[]{:S(2)}) %collective-permute-start.23) | collective-permute-done | bytes 589856 | tf_op jit(solution)/shard_map/ppermute | solution.py:251
  434.7 2.2 add_bitcast_fusion
  (137 shorter events, 37.3 us)
Async XLA Ops:
  0.6 93.2 %collective-permute-start.5 = (bf16[256,4608]{1,0:T(8,128)(2,1)}, bf16[256,4608]{1,0:T(8,128)(2,1)}, u32[]{:S(2)}, u32[]{:S(2)}) collective-permute-start(bf16[256,4608]{1,0:T(8,128)(2,1)} %param.9), channel_id=1, source_target_pairs={{0,1},{1,0},{2,3},{3,2},{4,5},{5,4},{6,7},{7,6},{8,9},{9,8},{10,11... | collective-permute-start | bytes 7077896 | tf_op jit(solution)/shard_map/ppermute | solution.py:191
  9.8 369.8 %copy-start.7 = (f32[512,64]{0,1:T(8,128)}, f32[512,64]{0,1:T(8,128)S(1)}, u32[]{:S(2)}) copy-start(f32[512,64]{0,1:T(8,128)S(1)} %get-tuple-element.57) | copy-start | bytes 393220
  10.0 1.0 copy-start.15
  12.4 7.1 %copy-start.14 = (bf16[1,512,512]{1,2,0:T(8,128)(2,1)S(1)}, bf16[1,512,512]{1,2,0:T(8,128)(2,1)}, u32[]{:S(2)}) copy-start(bf16[1,512,512]{1,2,0:T(8,128)(2,1)} %get-tuple-element.33) | copy-start | bytes 1572868
  14.5 15.1 %collective-permute-start = (bf16[1,512,512]{2,1,0:T(8,128)(2,1)}, bf16[1,512,512]{2,1,0:T(8,128)(2,1)}, u32[]{:S(2)}, u32[]{:S(2)}) collective-permute-start(bf16[1,512,512]{2,1,0:T(8,128)(2,1)} %bitcast.7), channel_id=1, source_target_pairs={{0,2},{2,4},{4,6},{6,0},{8,10},{10,12},{12,14},{14,8},{16,18},{18,... | collective-permute-start | bytes 1572872 | tf_op jit(solution)/shard_map/ppermute | solution.py:182
  15.5 25.4 %collective-permute-start.1 = (bf16[1,512,512]{2,1,0:T(8,128)(2,1)}, bf16[1,512,512]{2,1,0:T(8,128)(2,1)}, u32[]{:S(2)}, u32[]{:S(2)}) collective-permute-start(bf16[1,512,512]{2,1,0:T(8,128)(2,1)} %bitcast.8), channel_id=1, source_target_pairs={{0,4},{2,6},{4,0},{6,2},{8,12},{10,14},{12,8},{14,10},{16,20},{18,... | collective-permute-start | bytes 1572872 | tf_op jit(solution)/shard_map/ppermute | solution.py:182
  18.0 34.1 %collective-permute-start.2 = (bf16[1,512,512]{2,1,0:T(8,128)(2,1)}, bf16[1,512,512]{2,1,0:T(8,128)(2,1)}, u32[]{:S(2)}, u32[]{:S(2)}) collective-permute-start(bf16[1,512,512]{2,1,0:T(8,128)(2,1)} %bitcast.9), channel_id=1, source_target_pairs={{0,6},{2,0},{4,2},{6,4},{8,14},{10,8},{12,10},{14,12},{16,22},{18,... | collective-permute-start | bytes 1572872 | tf_op jit(solution)/shard_map/ppermute | solution.py:182
  64.1 32.4 %copy-start.5 = (bf16[2048,256]{0,1:T(8,128)(2,1)}, bf16[2048,256]{0,1:T(8,128)(2,1)S(1)}, u32[]{:S(2)}) copy-start(bf16[2048,256]{0,1:T(8,128)(2,1)S(1)} %get-tuple-element.28) | copy-start | bytes 3145732
  64.1 25.1 %collective-permute-start.3 = (bf16[2048,256]{0,1:T(8,128)(2,1)S(1)}, bf16[2048,256]{0,1:T(8,128)(2,1)S(1)}, u32[]{:S(2)}, u32[]{:S(2)}) collective-permute-start(bf16[2048,256]{0,1:T(8,128)(2,1)S(1)} %get-tuple-element.28), channel_id=1, source_target_pairs={{0,8},{2,10},{4,12},{6,14},{8,16},{10,18},{12,20},{14,22},{16,24},... | collective-permute-start | bytes 3145736 | tf_op jit(solution)/shard_map/ppermute | solution.py:188
  89.2 7.3 %copy-start.19 = (bf16[2048,256]{0,1:T(8,128)(2,1)}, bf16[2048,256]{0,1:T(8,128)(2,1)S(1)}, u32[]{:S(2)}) copy-start(bf16[2048,256]{0,1:T(8,128)(2,1)S(1)} %collective-permute-done.3) | copy-start | bytes 3145732
  89.2 25.1 %collective-permute-start.4 = (bf16[2048,256]{0,1:T(8,128)(2,1)S(1)}, bf16[2048,256]{0,1:T(8,128)(2,1)S(1)}, u32[]{:S(2)}, u32[]{:S(2)}) collective-permute-start(bf16[2048,256]{0,1:T(8,128)(2,1)S(1)} %collective-permute-done.3), channel_id=1, source_target_pairs={{0,8},{2,10},{4,12},{6,14},{8,16},{10,18},{12,20},{14,22},{16,24},... | collective-permute-start | bytes 3145736 | tf_op jit(solution)/shard_map/ppermute | solution.py:188
  96.6 11.5 %copy-start.9 = (bf16[256,4608]{1,0:T(8,128)(2,1)}, bf16[256,4608]{1,0:T(8,128)(2,1)S(1)}, u32[]{:S(2)}) copy-start(bf16[256,4608]{1,0:T(8,128)(2,1)S(1)} %get-tuple-element.22) | copy-start | bytes 7077892
  96.6 11.5 %copy-start.11 = (bf16[256,4608]{1,0:T(8,128)(2,1)}, bf16[256,4608]{1,0:T(8,128)(2,1)S(1)}, u32[]{:S(2)}) copy-start(bf16[256,4608]{1,0:T(8,128)(2,1)S(1)} %get-tuple-element.23) | copy-start | bytes 7077892
  96.6 17.7 %copy-start.6 = (bf16[2048,256]{0,1:T(8,128)(2,1)S(1)}, bf16[2048,256]{0,1:T(8,128)(2,1)}, u32[]{:S(2)}) copy-start(bf16[2048,256]{0,1:T(8,128)(2,1)} %copy-done.5) | copy-start | bytes 3145732
  96.6 17.7 %copy-start.20 = (bf16[2048,256]{0,1:T(8,128)(2,1)S(1)}, bf16[2048,256]{0,1:T(8,128)(2,1)}, u32[]{:S(2)}) copy-start(bf16[2048,256]{0,1:T(8,128)(2,1)} %copy-done.19) | copy-start | bytes 3145732
  114.6 3.3 copy-start
  134.3 3.0 copy-start.18
  137.3 10.7 %collective-permute-start.17 = (bf16[1,512,256]{1,2,0:T(8,128)(2,1)}, bf16[1,512,256]{1,2,0:T(8,128)(2,1)}, u32[]{:S(2)}, u32[]{:S(2)}) collective-permute-start(bf16[1,512,256]{1,2,0:T(8,128)(2,1)} %copy.91), channel_id=1, source_target_pairs={{0,2},{2,4},{4,6},{6,0},{8,10},{10,12},{12,14},{14,8},{16,18},{18,... | collective-permute-start | bytes 786440 | tf_op jit(solution)/shard_map/ppermute | solution.py:182
  139.1 10.6 %collective-permute-start.18 = (bf16[1,512,256]{1,2,0:T(8,128)(2,1)}, bf16[1,512,256]{1,2,0:T(8,128)(2,1)}, u32[]{:S(2)}, u32[]{:S(2)}) collective-permute-start(bf16[1,512,256]{1,2,0:T(8,128)(2,1)} %copy.92), channel_id=1, source_target_pairs={{0,4},{2,6},{4,0},{6,2},{8,12},{10,14},{12,8},{14,10},{16,20},{18,... | collective-permute-start | bytes 786440 | tf_op jit(solution)/shard_map/ppermute | solution.py:182
  142.4 17.3 %copy-start.10 = (bf16[256,4608]{1,0:T(8,128)(2,1)S(1)}, bf16[256,4608]{1,0:T(8,128)(2,1)}, u32[]{:S(2)}) copy-start(bf16[256,4608]{1,0:T(8,128)(2,1)} %copy-done.9) | copy-start | bytes 7077892
  143.1 45.4 %collective-permute-start.6 = (bf16[1,512,256]{1,2,0:T(8,128)(2,1)}, bf16[1,512,256]{1,2,0:T(8,128)(2,1)}, u32[]{:S(2)}, u32[]{:S(2)}) collective-permute-start(bf16[1,512,256]{1,2,0:T(8,128)(2,1)} %get-tuple-element.54), channel_id=1, source_target_pairs={{0,2},{2,4},{4,6},{6,0},{8,10},{10,12},{12,14},{14,8},{16,18},{18,... | collective-permute-start | bytes 786440 | tf_op jit(solution)/shard_map/ppermute | solution.py:182
  143.2 47.0 %collective-permute-start.7 = (bf16[1,512,256]{1,2,0:T(8,128)(2,1)}, bf16[1,512,256]{1,2,0:T(8,128)(2,1)S(1)}, u32[]{:S(2)}, u32[]{:S(2)}) collective-permute-start(bf16[1,512,256]{1,2,0:T(8,128)(2,1)} %get-tuple-element.53), channel_id=1, source_target_pairs={{0,4},{2,6},{4,0},{6,2},{8,12},{10,14},{12,8},{14,10},{16,20},{18,... | collective-permute-start | bytes 786440 | tf_op jit(solution)/shard_map/ppermute | solution.py:182
  147.9 11.8 %copy-start.12 = (bf16[256,4608]{1,0:T(8,128)(2,1)S(1)}, bf16[256,4608]{1,0:T(8,128)(2,1)}, u32[]{:S(2)}) copy-start(bf16[256,4608]{1,0:T(8,128)(2,1)} %copy-done.11) | copy-start | bytes 7077892
  147.9 11.7 %collective-permute-start.19 = (bf16[1,512,256]{1,2,0:T(8,128)(2,1)}, bf16[1,512,256]{1,2,0:T(8,128)(2,1)S(1)}, u32[]{:S(2)}, u32[]{:S(2)}) collective-permute-start(bf16[1,512,256]{1,2,0:T(8,128)(2,1)} %copy.93), channel_id=1, source_target_pairs={{0,6},{2,0},{4,2},{6,4},{8,14},{10,8},{12,10},{14,12},{16,22},{18,... | collective-permute-start | bytes 786440 | tf_op jit(solution)/shard_map/ppermute | solution.py:182
  148.0 42.9 %collective-permute-start.8 = (bf16[1,512,256]{1,2,0:T(8,128)(2,1)}, bf16[1,512,256]{1,2,0:T(8,128)(2,1)}, u32[]{:S(2)}, u32[]{:S(2)}) collective-permute-start(bf16[1,512,256]{1,2,0:T(8,128)(2,1)} %get-tuple-element.52), channel_id=1, source_target_pairs={{0,6},{2,0},{4,2},{6,4},{8,14},{10,8},{12,10},{14,12},{16,22},{18,... | collective-permute-start | bytes 786440 | tf_op jit(solution)/shard_map/ppermute | solution.py:182
  180.1 7.2 %copy-start.1 = (bf16[6144,256]{0,1:T(8,128)(2,1)S(1)}, bf16[6144,256]{0,1:T(8,128)(2,1)}, u32[]{:S(2)}) copy-start(bf16[6144,256]{0,1:T(8,128)(2,1)} %copy-done) | copy-start | bytes 9437188
  187.2 37.1 %collective-permute-start.20 = (bf16[8,8,8,4608]{3,2,1,0:T(8,128)(2,1)}, bf16[8,8,8,4608]{3,2,1,0:T(8,128)(2,1)}, u32[]{:S(2)}, u32[]{:S(2)}) collective-permute-start(bf16[8,8,8,4608]{3,2,1,0:T(8,128)(2,1)} %bitcast.77), channel_id=1, source_target_pairs={{0,2},{2,0},{4,6},{6,4},{8,10},{10,8},{12,14},{14,12},{16,18},{18,... | collective-permute-start | bytes 14155784 | tf_op jit(solution)/shard_map/ppermute | solution.py:251
  194.9 29.5 %slice-start = ((s8[4718592]{0:T(1024)(128)(4,1)}), s8[4194304]{0:T(1024)(128)(4,1)S(1)}, s32[]{:S(2)}) async-start(s8[4718592]{0:T(1024)(128)(4,1)} %bitcast.82), calls=%async_computation | async-start | bytes 8388608
  194.9 29.5 %slice-start.1 = ((s8[4718592]{0:T(1024)(128)(4,1)}), s8[524288]{0:T(1024)(128)(4,1)S(1)}, s32[]{:S(2)}) async-start(s8[4718592]{0:T(1024)(128)(4,1)} %bitcast.82), calls=%async_computation.1 | async-start | bytes 1048576
  221.1 73.0 %slice-start.2 = ((s8[6291456]{0:T(1024)(128)(4,1)}), s8[4194304]{0:T(1024)(128)(4,1)S(1)}, s32[]{:S(2)}) async-start(s8[6291456]{0:T(1024)(128)(4,1)} %bitcast.91), calls=%async_computation.2 | async-start | bytes 8388608
  222.9 71.2 %collective-permute-start.12 = (bf16[2048,256]{1,0:T(8,128)(2,1)S(1)}, bf16[2048,256]{1,0:T(8,128)(2,1)}, u32[]{:S(2)}, u32[]{:S(2)}) collective-permute-start(bf16[2048,256]{1,0:T(8,128)(2,1)S(1)} %slice.103), channel_id=1, source_target_pairs={{8,0},{10,2},{12,4},{14,6},{16,8},{18,10},{20,12},{22,14},{24,16},... | collective-permute-start | bytes 3145736 | tf_op jit(solution)/shard_map/ppermute | solution.py:188
  224.4 69.7 %slice-start.3 = ((s8[6291456]{0:T(1024)(128)(4,1)}), s8[2097152]{0:T(1024)(128)(4,1)S(1)}, s32[]{:S(2)}) async-start(s8[6291456]{0:T(1024)(128)(4,1)} %bitcast.91), calls=%async_computation.3 | async-start | bytes 4194304
  229.8 2.2 copy-start.2
  231.9 140.6 %collective-permute-start.21 = (bf16[4,8,8,4608]{3,2,1,0:T(8,128)(2,1)S(1)}, bf16[4,8,8,4608]{3,2,1,0:T(8,128)(2,1)}, u32[]{:S(2)}, u32[]{:S(2)}) collective-permute-start(bf16[4,8,8,4608]{3,2,1,0:T(8,128)(2,1)S(1)} %dynamic-slice_bitcast_fusion), channel_id=1, source_target_pairs={{0,4},{2,6},{4,0},{6,2},{8,12},{10,14},{12,8},{14,10},{16,20},{18,... | collective-permute-start | bytes 7077896 | tf_op jit(solution)/shard_map/ppermute | solution.py:251
  295.7 53.4 %copy-start.21 = (bf16[2048,256]{1,0:T(8,128)(2,1)S(1)}, bf16[2048,256]{1,0:T(8,128)(2,1)}, u32[]{:S(2)}) copy-start(bf16[2048,256]{1,0:T(8,128)(2,1)} %get-tuple-element.10) | copy-start | bytes 3145732
  295.7 53.1 %collective-permute-start.13 = (bf16[2048,256]{1,0:T(8,128)(2,1)S(1)}, bf16[2048,256]{1,0:T(8,128)(2,1)S(1)}, u32[]{:S(2)}, u32[]{:S(2)}) collective-permute-start(bf16[2048,256]{1,0:T(8,128)(2,1)S(1)} %add_convert_fusion.1), channel_id=1, source_target_pairs={{8,0},{10,2},{12,4},{14,6},{16,8},{18,10},{20,12},{22,14},{24,16},... | collective-permute-start | bytes 3145736 | tf_op jit(solution)/shard_map/ppermute | solution.py:188
  350.5 10.0 %copy-start.23 = (bf16[1,512,256]{2,1,0:T(8,128)(2,1)S(1)}, bf16[1,512,256]{2,1,0:T(8,128)(2,1)}, u32[]{:S(2)}) copy-start(bf16[1,512,256]{2,1,0:T(8,128)(2,1)} %get-tuple-element.47) | copy-start | bytes 786436
  350.5 10.8 %copy-start.22 = (bf16[1,512,256]{2,1,0:T(8,128)(2,1)S(1)}, bf16[1,512,256]{2,1,0:T(8,128)(2,1)}, u32[]{:S(2)}) copy-start(bf16[1,512,256]{2,1,0:T(8,128)(2,1)} %get-tuple-element.46) | copy-start | bytes 786436
  352.3 15.6 %collective-permute-start.9 = (bf16[1,512,256]{1,2,0:T(8,128)(2,1)}, bf16[1,512,256]{1,2,0:T(8,128)(2,1)}, u32[]{:S(2)}, u32[]{:S(2)}) collective-permute-start(bf16[1,512,256]{1,2,0:T(8,128)(2,1)} %copy.83), channel_id=1, source_target_pairs={{0,2},{2,4},{4,6},{6,0},{8,10},{10,12},{12,14},{14,8},{16,18},{18,... | collective-permute-start | bytes 786440 | tf_op jit(solution)/shard_map/ppermute | solution.py:182
  356.0 13.8 %collective-permute-start.10 = (bf16[1,512,256]{1,2,0:T(8,128)(2,1)}, bf16[1,512,256]{1,2,0:T(8,128)(2,1)}, u32[]{:S(2)}, u32[]{:S(2)}) collective-permute-start(bf16[1,512,256]{1,2,0:T(8,128)(2,1)} %copy.84), channel_id=1, source_target_pairs={{0,4},{2,6},{4,0},{6,2},{8,12},{10,14},{12,8},{14,10},{16,20},{18,... | collective-permute-start | bytes 786440 | tf_op jit(solution)/shard_map/ppermute | solution.py:182
  359.0 19.3 %collective-permute-start.11 = (bf16[1,512,256]{1,2,0:T(8,128)(2,1)}, bf16[1,512,256]{1,2,0:T(8,128)(2,1)}, u32[]{:S(2)}, u32[]{:S(2)}) collective-permute-start(bf16[1,512,256]{1,2,0:T(8,128)(2,1)} %copy.85), channel_id=1, source_target_pairs={{0,6},{2,0},{4,2},{6,4},{8,14},{10,8},{12,10},{14,12},{16,22},{18,... | collective-permute-start | bytes 786440 | tf_op jit(solution)/shard_map/ppermute | solution.py:182
  362.2 22.3 %collective-permute-start.14 = (bf16[1,512,256]{1,2,0:T(8,128)(2,1)}, bf16[1,512,256]{1,2,0:T(8,128)(2,1)}, u32[]{:S(2)}, u32[]{:S(2)}) collective-permute-start(bf16[1,512,256]{1,2,0:T(8,128)(2,1)} %copy.87), channel_id=1, source_target_pairs={{0,2},{2,4},{4,6},{6,0},{8,10},{10,12},{12,14},{14,8},{16,18},{18,... | collective-permute-start | bytes 786440 | tf_op jit(solution)/shard_map/ppermute | solution.py:182
  367.9 4.6 %copy-start.3 = (bf16[4,512,256]{1,2,0:T(8,128)(2,1)}, bf16[4,512,256]{1,2,0:T(8,128)(2,1)S(1)}, u32[]{:S(2)}) copy-start(bf16[4,512,256]{1,2,0:T(8,128)(2,1)S(1)} %constant_dynamic-update-slice_fusion.7) | copy-start | bytes 3145732
  367.9 17.6 %collective-permute-start.15 = (bf16[1,512,256]{1,2,0:T(8,128)(2,1)}, bf16[1,512,256]{1,2,0:T(8,128)(2,1)}, u32[]{:S(2)}, u32[]{:S(2)}) collective-permute-start(bf16[1,512,256]{1,2,0:T(8,128)(2,1)} %copy.88), channel_id=1, source_target_pairs={{0,4},{2,6},{4,0},{6,2},{8,12},{10,14},{12,8},{14,10},{16,20},{18,... | collective-permute-start | bytes 786440 | tf_op jit(solution)/shard_map/ppermute | solution.py:182
  369.8 16.7 %collective-permute-start.16 = (bf16[1,512,256]{1,2,0:T(8,128)(2,1)}, bf16[1,512,256]{1,2,0:T(8,128)(2,1)}, u32[]{:S(2)}, u32[]{:S(2)}) collective-permute-start(bf16[1,512,256]{1,2,0:T(8,128)(2,1)} %copy.89), channel_id=1, source_target_pairs={{0,6},{2,0},{4,2},{6,4},{8,14},{10,8},{12,10},{14,12},{16,22},{18,... | collective-permute-start | bytes 786440 | tf_op jit(solution)/shard_map/ppermute | solution.py:182
  376.6 3.0 copy-start.16
  376.6 27.8 %collective-permute-start.22 = (bf16[2,8,8,4608]{3,2,1,0:T(8,128)(2,1)}, bf16[2,8,8,4608]{3,2,1,0:T(8,128)(2,1)}, u32[]{:S(2)}, u32[]{:S(2)}) collective-permute-start(bf16[2,8,8,4608]{3,2,1,0:T(8,128)(2,1)} %dynamic-slice_bitcast_fusion.1), channel_id=1, source_target_pairs={{0,8},{2,10},{4,12},{6,14},{8,0},{10,2},{12,4},{14,6},{16,24},{18,... | collective-permute-start | bytes 3538952 | tf_op jit(solution)/shard_map/ppermute | solution.py:251
  381.5 3.0 copy-start.4
  388.4 21.0 %copy-start.8 = (f32[512,64]{0,1:T(8,128)S(1)}, f32[512,64]{0,1:T(8,128)}, u32[]{:S(2)}) copy-start(f32[512,64]{0,1:T(8,128)} %copy-done.7) | copy-start | bytes 393220
  388.4 21.0 %copy-start.17 = (f32[512,64]{0,1:T(8,128)S(1)}, f32[512,64]{0,1:T(8,128)}, u32[]{:S(2)}) copy-start(f32[512,64]{0,1:T(8,128)} %get-tuple-element.55) | copy-start | bytes 393220
  406.8 27.8 %collective-permute-start.23 = (bf16[1,8,8,4608]{3,2,1,0:T(8,128)(2,1)}, bf16[1,8,8,4608]{3,2,1,0:T(8,128)(2,1)}, u32[]{:S(2)}, u32[]{:S(2)}) collective-permute-start(bf16[1,8,8,4608]{3,2,1,0:T(8,128)(2,1)} %constant_dynamic-slice_fusion.14), channel_id=1, source_target_pairs={{0,16},{2,18},{4,20},{6,22},{8,24},{10,26},{12,28},{14,30},{16,0},... | collective-permute-start | bytes 1769480 | tf_op jit(solution)/shard_map/ppermute | solution.py:251
  409.6 1.4 copy-start.13
